TPU v7x, 32 devices: a whole 2x2x4 slice. The times are simulated.
32 devices in a mesh: groups: 2 (over x), dp: 8 (over z, y), tensor: 2 (over core).
Axes of the slice: x: 2, y: 2, z: 4, core: 2. Of those that a mesh axis runs over, the one named last changes fastest.
Arguments:
- train_hidden: bfloat16 [32, 256, 14336], P(('groups', 'dp'), None, 'tensor'), parts along dimension 0, may hold values from -6 to 6
- train_outgrad: bfloat16 [32, 256, 4096], P(('groups', 'dp'), None, 'tensor'), parts along dimension 0, may hold values from -6 to 6
- train_padding: int32 [32], P(('groups', 'dp')), parts along dimension 0, may hold values from 0 to 128
- query_hidden: bfloat16 [32, 64, 14336], P(('groups', 'dp'), None, 'tensor'), parts along dimension 0, may hold values from -6 to 6
- query_outgrad: bfloat16 [32, 64, 4096], P(('groups', 'dp'), None, 'tensor'), parts along dimension 0, may hold values from -6 to 6
- query_padding: int32 [32], P(('groups', 'dp')), parts along dimension 0, may hold values from 0 to 32
- proj_in: bfloat16 [64, 14336], P(None, 'tensor'), may hold values from -0.046875 to 0.046875
- output_projection: bfloat16 [64, 4096], P(None, 'tensor'), may hold values from -0.09375 to 0.09375
- in_inverse: float32 [64, 64], replicated, may hold values from -0.2 to 2.2, as said below
- output_inverse: float32 [64, 64], replicated, may hold values from -0.2 to 2.2, as said below
Outputs:
- scores: float32 [32, 16], P(('groups', 'dp')), parts along dimension 0
There are 2 independent parts, one for each index of `groups`. A program takes and returns all parts, laid end to end along the dimension named above; an argument that names none is the same for every part. Nothing has to cross between parts.
Inputs may be any that keep to these rules, and one draw needn't show every extreme that they name: `in_inverse`: a given inverse factor. `output_inverse`: a given inverse factor.
All inputs are finite; a program needn't handle non-finite values.
Results may differ from a plain program's by a relative error of at most 0.0003.
Values sent between devices are 32-bit elements; how exact they have to be, the bound alone decides.
A program may use at most 64 MiB of HBM per device.

v0:
```python
import jax
import jax.numpy as jnp
from jax import lax
from jax.sharding import PartitionSpec as P

HIGH = lax.Precision.HIGHEST


def input_side(hidden, proj_in):
    return jnp.einsum("kf,slf->skl", proj_in, hidden, preferred_element_type=jnp.float32)


def output_side(output_gradient, output_projection):
    return jnp.einsum(
        "wy,miy->mwi", output_projection, output_gradient, preferred_element_type=jnp.float32
    )


def outer_blocks(output_facing, padding_mask, in_side):
    length = output_facing.shape[2]
    positions = jnp.arange(length, dtype=jnp.int32)
    validity = (positions[None, :] < (length - padding_mask)[:, None]).astype(jnp.float32)
    counted_tokens = (length - padding_mask).astype(jnp.float32)
    weighted = output_facing * (validity / counted_tokens[:, None])[:, None, :]
    return jnp.einsum("skl,sjl->skj", weighted, in_side, precision=HIGH)


def on_device(
    train_hidden,
    train_outgrad,
    train_padding,
    query_hidden,
    query_outgrad,
    query_padding,
    proj_in,
    output_projection,
    in_inverse,
    output_inverse,
):
    train_part = input_side(train_hidden, proj_in)
    query_part = input_side(query_hidden, proj_in)
    train_facing = output_side(train_outgrad, output_projection)
    query_facing = output_side(query_outgrad, output_projection)
    train_in, query_in, train_out, query_out = lax.psum(
        (train_part, query_part, train_facing, query_facing), "tensor"
    )
    train_blocks = outer_blocks(train_out, train_padding, train_in)
    query_blocks = outer_blocks(query_out, query_padding, query_in)
    left = jnp.einsum("ij,qjk->qik", output_inverse, query_blocks, precision=HIGH)
    conditioned_factor = jnp.einsum("qik,kl->qil", left, in_inverse, precision=HIGH)
    train_flat = train_blocks.reshape(train_blocks.shape[0], -1)
    query_flat = conditioned_factor.reshape(conditioned_factor.shape[0], -1)
    return jnp.dot(
        train_flat, lax.all_gather(query_flat, "dp", axis=0, tiled=True).T, precision=HIGH
    )


def solution(mesh):
    in_specs = (
        P(("groups", "dp"), None, "tensor"),
        P(("groups", "dp"), None, "tensor"),
        P(("groups", "dp")),
        P(("groups", "dp"), None, "tensor"),
        P(("groups", "dp"), None, "tensor"),
        P(("groups", "dp")),
        P(None, "tensor"),
        P(None, "tensor"),
        P(),
        P(),
    )
    out_specs = P(("groups", "dp"), None)
    return jax.shard_map(
        on_device, mesh=mesh, in_specs=in_specs, out_specs=out_specs, check_vma=False
    )
```

profile of v0, /device:TPU:0, one launch (start us, length us, event | category | flops | bytes accessed | tf_op | source)
XLA Modules:
  0.0 73.7 jit_solution(17574124622732042138)
XLA Ops:
  6.5 0.0 copy-start
  6.5 0.0 copy-start.1
  6.5 0.0 copy-start.2
  6.5 0.0 all-reduce.5.cloned.1.call-start
  6.5 0.0 copy-start.3
  6.6 3.1 %convolution_bitcast_fusion.3 = f32[2,64,64]{1,2,0:T(8,128)} fusion(bf16[2,64,7168]{2,1,0:T(8,128)(2,1)} %param.13, bf16[64,7168]{1,0:T(8,128)(2,1)} %param.16), kind=kOutput, calls=%fused_computation.3 | convolution fusion | flops 117440512 | bytes 2785280 | tf_op jit(solution)/shard_map/kf,slf->skl/dot_general | solution.py:10
  9.7 0.0 copy-done.2
  9.7 0.0 copy-done.3
  9.7 0.9 %convolution_bitcast_fusion.4 = f32[2,64,64]{1,2,0:T(8,128)} fusion(bf16[2,64,2048]{2,1,0:T(8,128)(2,1)S(1)} %copy-done.3, bf16[64,2048]{1,0:T(8,128)(2,1)S(1)} %copy-done.2), kind=kOutput, calls=%fused_computation.4 | convolution fusion | flops 33554432 | bytes 819200 | tf_op jit(solution)/shard_map/wy,miy->mwi/dot_general | solution.py:14
  10.6 0.0 all-reduce.5.cloned.1.call-update
  10.6 0.0 all-reduce.7.cloned.1.call-start
  10.7 0.0 copy-done.1
  10.7 6.1 %convolution_bitcast_fusion = f32[2,64,256]{2,1,0:T(8,128)} fusion(bf16[2,256,7168]{2,1,0:T(8,128)(2,1)} %param.10, bf16[64,7168]{1,0:T(8,128)(2,1)S(1)} %copy-done.1), kind=kOutput, calls=%fused_computation | convolution fusion | flops 469762048 | bytes 8388608 | tf_op jit(solution)/shard_map/kf,slf->skl/dot_general | solution.py:10
  16.8 0.0 copy-done
  16.8 0.0 copy-start.6
  16.8 0.0 copy-start.7
  16.8 0.0 copy-start.4
  16.8 0.0 copy-start.5
  16.8 1.4 %convolution_bitcast_fusion.1 = f32[2,64,256]{2,1,0:T(8,128)} fusion(bf16[2,256,2048]{2,1,0:T(8,128)(2,1)S(1)} %copy-done, bf16[64,2048]{1,0:T(8,128)(2,1)S(1)} %copy-done.2), kind=kOutput, calls=%fused_computation.1 | convolution fusion | flops 134217728 | bytes 2490368 | tf_op jit(solution)/shard_map/wy,miy->mwi/dot_general | solution.py:14
  18.2 0.0 all-reduce.7.cloned.1.call-update
  18.2 0.0 copy-done.6
  18.3 0.0 copy-done.7
  18.3 0.1 fusion.13
  18.4 0.1 fusion.14
  18.4 13.1 %all-reduce.5.cloned.1.call-done = (f32[2,64,64]{1,2,0:T(8,128)}, f32[2,64,64]{1,2,0:T(8,128)}) async-done(((f32[2,64,64]{1,2,0:T(8,128)}, f32[2,64,64]{1,2,0:T(8,128)}), (f32[2,64,64]{1,2,0:T(8,128)}, f32[2,64,64]{1,2,0:T(8,128)})) %all-reduce.5.cloned.1.call-update) | async-done | bytes 65552 | tf_op jit(solution)/shard_map/psum | solution.py:44
  31.5 1.2 %fusion.6 = f32[2,64,64]{2,1,0:T(8,128)S(1)} fusion(f32[2,64,64]{1,2,0:T(8,128)} %get-tuple-element.5, f32[2,64,64]{1,2,0:T(8,128)} %get-tuple-element.6, f32[2,64]{1,0:T(2,128)S(1)} %fusion.14), kind=kOutput, calls=%fused_computation.11 | convolution fusion | flops 6299648 | bytes 98816 | tf_op jit(solution)/shard_map/skl,sjl->skj/dot_general | solution.py:25
  32.8 0.0 copy-done.4
  32.8 0.2 convolution_bitcast_fusion.2
  33.0 0.0 copy-done.5
  33.0 0.2 fusion.9
  33.2 0.1 reshape.68
  33.3 31.1 %all-gather = f32[8,2,4096]{2,1,0:T(2,128)S(1)} all-gather(f32[1,2,4096]{2,1,0:T(2,128)S(1)} %reshape.68), channel_id=1, replica_groups=mesh['groups'=2,'dp'=8,'tensor'=2] {'dp'}, dimensions={0}, use_global_device_ids=true | all-gather | bytes 294912 | tf_op jit(solution)/shard_map/all_gather | solution.py:54
  64.4 0.2 reshape.69
  64.6 0.0 all-reduce.7.cloned.1.call-done
  64.6 1.2 %fusion.4 = f32[2,64,64]{2,1,0:T(8,128)S(1)} fusion(f32[2,64,256]{2,1,0:T(8,128)} %get-tuple-element.7, f32[2,64,256]{2,1,0:T(8,128)} %get-tuple-element.8, f32[2,256]{1,0:T(2,128)S(1)} %fusion.13), kind=kOutput, calls=%fused_computation.9 | convolution fusion | flops 25198592 | bytes 296960 | tf_op jit(solution)/shard_map/skl,sjl->skj/dot_general | solution.py:25
  65.8 0.1 reshape.66
  65.9 1.0 %fusion.17 = f32[2,16]{1,0:T(2,128)} fusion(f32[2,4096]{1,0:T(2,128)S(1)} %reshape.66, f32[16,4096]{1,0:T(8,128)S(1)} %reshape.69), kind=kOutput, calls=%fused_computation.26 | convolution fusion | flops 1572864 | bytes 295040 | tf_op jit(solution)/shard_map/dot_general | solution.py:53
  (2 shorter events, 0.0 us)
Async XLA Ops:
  6.5 10.2 %copy-start = (bf16[2,256,2048]{2,1,0:T(8,128)(2,1)S(1)}, bf16[2,256,2048]{2,1,0:T(8,128)(2,1)}, u32[]{:S(2)}) copy-start(bf16[2,256,2048]{2,1,0:T(8,128)(2,1)} %param.11) | copy-start | bytes 6291460
  6.5 4.2 %copy-start.1 = (bf16[64,7168]{1,0:T(8,128)(2,1)S(1)}, bf16[64,7168]{1,0:T(8,128)(2,1)}, u32[]{:S(2)}) copy-start(bf16[64,7168]{1,0:T(8,128)(2,1)} %param.16) | copy-start | bytes 2752516
  6.5 3.1 %copy-start.2 = (bf16[64,2048]{1,0:T(8,128)(2,1)S(1)}, bf16[64,2048]{1,0:T(8,128)(2,1)}, u32[]{:S(2)}) copy-start(bf16[64,2048]{1,0:T(8,128)(2,1)} %param.17) | copy-start | bytes 786436
  6.5 25.0 %all-reduce.5.cloned.1.call-start = ((), (), s32[]{:S(2)}) async-start(), calls=%async_computation | async-start | bytes 262144 | tf_op jit(solution)/shard_map/psum | solution.py:44
  6.5 3.1 %copy-start.3 = (bf16[2,64,2048]{2,1,0:T(8,128)(2,1)S(1)}, bf16[2,64,2048]{2,1,0:T(8,128)(2,1)}, u32[]{:S(2)}) copy-start(bf16[2,64,2048]{2,1,0:T(8,128)(2,1)} %param.14) | copy-start | bytes 1572868
  10.6 54.0 %all-reduce.7.cloned.1.call-start = ((), (), s32[]{:S(2)}) async-start(), calls=%async_computation.1 | async-start | bytes 524288 | tf_op jit(solution)/shard_map/psum | solution.py:44
  16.8 1.5 %copy-start.6 = (s32[2]{0:T(128)S(1)}, s32[2]{0:T(128)}, u32[]{:S(2)}) copy-start(s32[2]{0:T(128)} %param.12) | copy-start | bytes 28
  16.8 1.5 %copy-start.7 = (s32[2]{0:T(128)S(1)}, s32[2]{0:T(128)}, u32[]{:S(2)}) copy-start(s32[2]{0:T(128)} %param.15) | copy-start | bytes 28
  16.8 16.0 %copy-start.4 = (f32[64,64]{1,0:T(8,128)S(1)}, f32[64,64]{1,0:T(8,128)}, u32[]{:S(2)}) copy-start(f32[64,64]{1,0:T(8,128)} %param.19) | copy-start | bytes 49156
  16.8 16.2 %copy-start.5 = (f32[64,64]{1,0:T(8,128)S(1)}, f32[64,64]{1,0:T(8,128)}, u32[]{:S(2)}) copy-start(f32[64,64]{1,0:T(8,128)} %param.18) | copy-start | bytes 49156
Sparse Core Ops, SparseCore 0:
  10.8 20.7 all-reduce.4
  33.9 19.4 all-reduce.6
where the time goes:
time: 74 us; the launch traced here: 73.7 us
  blocking collectives  31.1 us (42%)
  matrix products  15.4 us (21%)
  between operations  13.5 us (18%)
  waiting for transfers between devices  13.1 us (18%)
    all_gather x1, blocking collectives, on_device(): lax.all_gather(query_flat, 'dp', axis=0, tiled=True)  31.1 us
    psum x2, waiting for transfers between devices, on_device(): lax.psum((train_part, query_part, train_facing, query_facing), 'tensor')  13.1 us
    dot_general x2, matrix products, input_side(): jnp.einsum('kf,slf->skl', proj_in, hidden, preferred_element_type=jnp.flo...  9.2 us
    dot_general x2, matrix products, outer_blocks(): return jnp.einsum('skl,sjl->skj', weighted, in_side, precision=HIGH)  2.46 us
    dot_general x2, matrix products, output_side(): jnp.einsum('wy,miy->mwi', output_projection, output_gradient, preferred_e...  2.33 us
  transfers between devices with their start and end apart: 2, of which 1 were waited for; matrix products, arithmetic and copies ran while one was open for 13% of the time, Pallas kernels for 0%

commit v1 on v0

v1 whole, which is shorter than its diff:
```python
import functools

import jax
import jax.numpy as jnp
from jax import lax
from jax.experimental import pallas as pl
from jax.experimental.pallas import tpu as pltpu
from jax.sharding import PartitionSpec as P

F32 = jnp.float32
BF16 = jnp.bfloat16
NT = (((1,), (1,)), ((), ()))
TN = (((0,), (0,)), ((), ()))
NN = (((1,), (0,)), ((), ()))


def dot(a, b, dims):
    return lax.dot_general(a, b, dims, preferred_element_type=F32)


def halves(x):
    high = x.astype(BF16)
    return high, (x - high.astype(F32)).astype(BF16)


def dot32(a, b, dims):
    a_high, a_low = halves(a)
    b_high, b_low = halves(b)
    return dot(a_high, b_high, dims) + (dot(a_high, b_low, dims) + dot(a_low, b_high, dims))


def outer(out_side, in_side):
    width = out_side.shape[1]
    left = jnp.concatenate(halves(out_side), axis=1)
    right = jnp.concatenate(halves(in_side), axis=1)
    full = dot(left, right, TN)
    return full[:width, :width] + (full[:width, width:] + full[width:, :width])


def pack(x):
    half = x.shape[0] // 2
    return jnp.concatenate([x[:half], x[half:]], axis=1)


def unpack(x):
    half = x.shape[1] // 2
    return jnp.concatenate([x[:, :half], x[:, half:]], axis=0)


def token_weights(tokens, first, length, padding):
    position = first + lax.broadcasted_iota(jnp.int32, (tokens, 1), 0)
    count = jnp.full((tokens, 1), length - padding, jnp.int32)
    return jnp.where(position < count, 1.0 / count.astype(F32), 0.0)


def kernel(
    n,
    chunk,
    th, tg, tp, qh, qg, qp, pi, po, ii, oi,
    out,
    th_v, tg_v, tp_s, qh_v, qg_v, qp_s, pi_v, po_v, ii_v, oi_v,
    q_mine, q_send, q_recv,
    o_send, o_recv, i_send, i_recv, gathered,
    load_sem, h_sem, ex_send, ex_recv, o_ssem, o_rsem, i_ssem, i_rsem,
    g_ssem, g_rsem, f_ssem, f_rsem,
):
    seqs, length, _ = th.shape
    queries, q_length, _ = qh.shape
    chunks = length // chunk
    me = lax.axis_index("dp")
    core = lax.axis_index("tensor")
    other = 1 - core

    def load(src, dst, k):
        copy = pltpu.make_async_copy(src, dst, load_sem.at[k])
        copy.start()
        return copy

    load_po = load(po, po_v, 0)
    load_qg = load(qg, qg_v, 1)
    load_pi = load(pi, pi_v, 2)
    load_qh = load(qh, qh_v, 3)
    load_qp = load(qp, qp_s, 4)
    load_tp = load(tp, tp_s, 5)
    load_oi = load(oi, oi_v, 6)
    load_ii = load(ii, ii_v, 7)
    load_tg = load(tg, tg_v, 8)
    load_th = []
    for s in range(seqs):
        for j in range(chunks):
            rows = pl.ds(j * chunk, chunk)
            copy = pltpu.make_async_copy(th.at[s, rows], th_v.at[s, rows], h_sem.at[s, j])
            copy.start()
            load_th.append(copy)

    barrier = pltpu.get_barrier_semaphore()
    for k in range(1, n):
        pl.semaphore_signal(barrier, inc=1, device_id={"dp": lax.rem(me + k, n)})
    pl.semaphore_signal(barrier, inc=1, device_id={"tensor": other})

    pending = []

    def send(src, dst, ssem, rsem, where):
        copy = pltpu.make_async_remote_copy(
            src_ref=src, dst_ref=dst, send_sem=ssem, recv_sem=rsem, device_id=where
        )
        copy.start()
        pending.append(copy)
        return copy

    load_po.wait()
    load_qg.wait()
    q_out = dot(qg_v[...].reshape(queries * q_length, -1), po_v[...], NT)
    load_pi.wait()
    load_qh.wait()
    q_in = dot(qh_v[...].reshape(queries * q_length, -1), pi_v[...], NT)
    q_both = jnp.concatenate([q_in, q_out], axis=1)
    first, second = q_both[:q_length], q_both[q_length:]
    q_send[...] = jnp.where(core == 0, second, first)
    q_mine[...] = jnp.where(core == 0, first, second)
    pl.semaphore_wait(barrier, n)
    ex_q = send(q_send, q_recv, ex_send, ex_recv, {"tensor": other})

    load_tg.wait()
    ex_o = []
    for s in range(seqs):
        o_send[s] = pack(dot(tg_v[s], po_v[...], NT))
        ex_o.append(send(o_send.at[s], o_recv.at[s], o_ssem.at[s], o_rsem.at[s], {"tensor": other}))

    width = pi.shape[0]
    load_qp.wait()
    load_oi.wait()
    load_ii.wait()
    ex_q.wait_recv()
    total = q_mine[...] + q_recv[...]
    padding = jnp.where(core == 0, qp_s[0], qp_s[1])
    weights = token_weights(q_length, 0, q_length, padding)
    block = outer(total[:, width:] * weights, total[:, :width])
    conditioned = dot32(dot32(oi_v[...], block, NN), ii_v[...], NN)
    slot = me * queries + core
    gathered[slot] = pack(conditioned)
    ex_g = []
    for k in range(1, n):
        ex_g.append(
            send(gathered.at[slot], gathered.at[slot], g_ssem.at[k], g_rsem.at[k], {"dp": lax.rem(me + k, n)})
        )
    ex_f = [send(gathered.at[slot], gathered.at[slot], f_ssem.at[0], f_rsem.at[0], {"tensor": other})]

    def pass_on(k):
        ex_g[k - 1].wait_recv()
        source = lax.rem(me + (n - k), n) * queries + core
        ex_f.append(
            send(gathered.at[source], gathered.at[source], f_ssem.at[k], f_rsem.at[k], {"tensor": other})
        )

    ex_i = []
    for s in range(seqs):
        for j in range(chunks):
            load_th[s * chunks + j].wait()
            i_send[s, j] = pack(dot(th_v[s, pl.ds(j * chunk, chunk), :], pi_v[...], NT))
            ex_i.append(
                send(i_send.at[s, j], i_recv.at[s, j], i_ssem.at[s, j], i_rsem.at[s, j], {"tensor": other})
            )
    for k in range(1, n):
        pass_on(k)

    load_tp.wait()
    facing = []
    for s in range(seqs):
        ex_o[s].wait_recv()
        weights = token_weights(length, 0, length, tp_s[s])
        facing.append(unpack(o_send[s] + o_recv[s]) * weights)

    ones = jnp.ones((8, 2 * width), BF16)
    for s in range(seqs):
        block = jnp.zeros((width, width), F32)
        for j in range(chunks):
            ex_i[s * chunks + j].wait_recv()
            in_side = unpack(i_send[s, j] + i_recv[s, j])
            block += outer(facing[s][j * chunk : (j + 1) * chunk], in_side)
        if s == 0:
            for copy in ex_f:
                copy.wait_recv()
        sums = jnp.sum(gathered[...] * pack(block)[None], axis=1)
        high, low = halves(sums)
        out[pl.ds(s, 1), :] = (dot(ones, high, NT) + dot(ones, low, NT))[:1]

    for copy in pending:
        copy.wait_send()


def on_device(n, th, tg, tp, qh, qg, qp, pi, po, ii, oi):
    seqs, length, ff = th.shape
    queries, q_length, _ = qh.shape
    width = pi.shape[0]
    chunk = 128
    chunks = length // chunk
    dma = pltpu.SemaphoreType.DMA
    hbm = pl.BlockSpec(memory_space=pl.ANY)
    return pl.pallas_call(
        functools.partial(kernel, n, chunk),
        out_shape=jax.ShapeDtypeStruct((seqs, n * queries), F32),
        in_specs=[hbm] * 10,
        out_specs=pl.BlockSpec(memory_space=pltpu.VMEM),
        scratch_shapes=[
            pltpu.VMEM(th.shape, BF16),
            pltpu.VMEM(tg.shape, BF16),
            pltpu.SMEM(tp.shape, jnp.int32),
            pltpu.VMEM(qh.shape, BF16),
            pltpu.VMEM(qg.shape, BF16),
            pltpu.SMEM(qp.shape, jnp.int32),
            pltpu.VMEM(pi.shape, BF16),
            pltpu.VMEM(po.shape, BF16),
            pltpu.VMEM(ii.shape, F32),
            pltpu.VMEM(oi.shape, F32),
            pltpu.VMEM((q_length, 2 * width), F32),
            pltpu.VMEM((q_length, 2 * width), F32),
            pltpu.VMEM((q_length, 2 * width), F32),
            pltpu.VMEM((seqs, length // 2, 2 * width), F32),
            pltpu.VMEM((seqs, length // 2, 2 * width), F32),
            pltpu.VMEM((seqs, chunks, chunk // 2, 2 * width), F32),
            pltpu.VMEM((seqs, chunks, chunk // 2, 2 * width), F32),
            pltpu.VMEM((n * queries, width // 2, 2 * width), F32),
            dma((9,)),
            dma((seqs, chunks)),
            dma,
            dma,
            dma((seqs,)),
            dma((seqs,)),
            dma((seqs, chunks)),
            dma((seqs, chunks)),
            dma((n,)),
            dma((n,)),
            dma((n,)),
            dma((n,)),
        ],
        compiler_params=pltpu.CompilerParams(
            collective_id=0, has_side_effects=True, vmem_limit_bytes=56 * 1024 * 1024
        ),
        cost_estimate=pl.CostEstimate(
            flops=2 * width * (seqs * length + queries * q_length) * (ff + tg.shape[2]),
            bytes_accessed=2 * (seqs * length + queries * q_length) * (ff + tg.shape[2]),
            transcendentals=0,
        ),
    )(th, tg, tp, qh, qg, qp, pi, po, ii, oi)


def solution(mesh):
    rows = ("groups", "dp")
    in_specs = (
        P(rows, None, "tensor"),
        P(rows, None, "tensor"),
        P(rows),
        P(rows, None, "tensor"),
        P(rows, None, "tensor"),
        P(rows),
        P(None, "tensor"),
        P(None, "tensor"),
        P(),
        P(),
    )
    return jax.shard_map(
        functools.partial(on_device, mesh.shape["dp"]),
        mesh=mesh,
        in_specs=in_specs,
        out_specs=P(rows, None),
        check_vma=False,
    )
```

time: 74 us -> 19.2 us (0.26)
  blocking collectives: 31.1 us -> 0 us
  Pallas kernels: 0 us -> 17.8 us
  matrix products: 15.4 us -> 0 us
  between operations: 13.5 us -> 0.01 us
  waiting for transfers between devices: 13.1 us -> 0 us
  local copies, waits for them, and re-layouts: 0.4 us -> 1.24 us
    all_gather x1 -> x0, blocking collectives: 31.1 us -> none  [on_device(): lax.all_gather(query_flat, 'dp', axis=0, tiled=True)]
    pallas_call x0 -> x1, Pallas kernels: none -> 17.8 us  [on_device(): pl.pallas_call(functools.partial(kernel, n, chunk), out_shape=jax.ShapeDt...]
    dot_general x9 -> x0, matrix products: 15.4 us -> none  [the longest x2 9.2 us: input_side(): jnp.einsum('kf,slf->skl', proj_in, hidden, preferred_element_type=jnp.flo...]
    psum x2 -> x0, waiting for transfers between devices: 13.1 us -> none  [on_device(): lax.psum((train_part, query_part, train_facing, query_facing), 'tensor')]
    unnamed x18 -> x1, local copies, waits for them, and re-layouts: 0.31 us -> 1.24 us
  transfers between devices with their start and end apart: 2 -> 0, of which waited for: 1 -> 0; matrix products, arithmetic and copies ran while one was open for 13% -> 0% of each run, Pallas kernels for 0% -> 0%
where the time goes in v1:
time: 19.2 us; the launch traced here: 19.1 us
  Pallas kernels  17.8 us (93%)
  local copies, waits for them, and re-layouts  1.24 us (6%)
    pallas_call x1, Pallas kernels, on_device(): pl.pallas_call(functools.partial(kernel, n, chunk), out_shape=jax.ShapeDt...  17.8 us
    unnamed x1, local copies, waits for them, and re-layouts  1.24 us

profile of v1, /device:TPU:0, one launch (start us, length us, event | category | flops | bytes accessed | tf_op | source)
XLA Modules:
  0.0 19.1 jit_solution(5296734941103167339)
XLA Ops:
  0.0 17.8 %shard_map.100 = f32[2,16]{1,0:T(2,128)} custom-call(bf16[2,256,7168]{2,1,0:T(8,128)(2,1)} %th.1, bf16[2,256,2048]{2,1,0:T(8,128)(2,1)} %tg.1, s32[2]{0:T(128)} %tp.1, bf16[2,64,7168]{2,1,0:T(8,128)(2,1)} %qh.1, bf16[2,64,2048]{2,1,0:T(8,128)(2,1)} %qg.1, s32[2]{0:T(128)} %qp.1, bf16[64,7168]{1,0:T(8,128)(2,1)} %pi.1, bf16[64,2048]{1,0:T(8,128)(2,1)} %po.1, ...), custom_call_target="tpu_custom_call" | custom-call | flops 754974720 | bytes 11796480 | tf_op jit(solution)/shard_map/pallas_call | solution.py:200
  17.8 1.2 %copy.12 = f32[2,16]{1,0:T(2,128)} copy(f32[2,16]{1,0:T(2,128)} %shard_map.100) | data formatting | bytes 256

commit v2 on v1

--- a/solution.py
+++ b/solution.py
@@ -84,15 +84,6 @@
     load_tp = load(tp, tp_s, 5)
     load_oi = load(oi, oi_v, 6)
     load_ii = load(ii, ii_v, 7)
-    load_tg = load(tg, tg_v, 8)
-    load_th = []
-    for s in range(seqs):
-        for j in range(chunks):
-            rows = pl.ds(j * chunk, chunk)
-            copy = pltpu.make_async_copy(th.at[s, rows], th_v.at[s, rows], h_sem.at[s, j])
-            copy.start()
-            load_th.append(copy)
-
     barrier = pltpu.get_barrier_semaphore()
     for k in range(1, n):
         pl.semaphore_signal(barrier, inc=1, device_id={"dp": lax.rem(me + k, n)})
@@ -113,6 +104,15 @@
     q_out = dot(qg_v[...].reshape(queries * q_length, -1), po_v[...], NT)
     load_pi.wait()
     load_qh.wait()
+    load_tg = load(tg, tg_v, 8)
+    load_th = []
+    for s in range(seqs):
+        for j in range(chunks):
+            rows = pl.ds(j * chunk, chunk)
+            copy = pltpu.make_async_copy(th.at[s, rows], th_v.at[s, rows], h_sem.at[s, j])
+            copy.start()
+            load_th.append(copy)
+
     q_in = dot(qh_v[...].reshape(queries * q_length, -1), pi_v[...], NT)
     q_both = jnp.concatenate([q_in, q_out], axis=1)
     first, second = q_both[:q_length], q_both[q_length:]
@@ -120,12 +120,6 @@
     q_mine[...] = jnp.where(core == 0, first, second)
     pl.semaphore_wait(barrier, n)
     ex_q = send(q_send, q_recv, ex_send, ex_recv, {"tensor": other})
-
-    load_tg.wait()
-    ex_o = []
-    for s in range(seqs):
-        o_send[s] = pack(dot(tg_v[s], po_v[...], NT))
-        ex_o.append(send(o_send.at[s], o_recv.at[s], o_ssem.at[s], o_rsem.at[s], {"tensor": other}))
 
     width = pi.shape[0]
     load_qp.wait()
@@ -153,6 +147,12 @@
             send(gathered.at[source], gathered.at[source], f_ssem.at[k], f_rsem.at[k], {"tensor": other})
         )
 
+    load_tg.wait()
+    ex_o = []
+    for s in range(seqs):
+        o_send[s] = pack(dot(tg_v[s], po_v[...], NT))
+        ex_o.append(send(o_send.at[s], o_recv.at[s], o_ssem.at[s], o_rsem.at[s], {"tensor": other}))
+
     ex_i = []
     for s in range(seqs):
         for j in range(chunks):
@@ -161,15 +161,15 @@
             ex_i.append(
                 send(i_send.at[s, j], i_recv.at[s, j], i_ssem.at[s, j], i_rsem.at[s, j], {"tensor": other})
             )
-    for k in range(1, n):
-        pass_on(k)
-
     load_tp.wait()
     facing = []
     for s in range(seqs):
         ex_o[s].wait_recv()
         weights = token_weights(length, 0, length, tp_s[s])
         facing.append(unpack(o_send[s] + o_recv[s]) * weights)
+
+    for k in range(1, n):
+        pass_on(k)
 
     ones = jnp.ones((8, 2 * width), BF16)
     for s in range(seqs):
@@ -193,7 +193,7 @@
     seqs, length, ff = th.shape
     queries, q_length, _ = qh.shape
     width = pi.shape[0]
-    chunk = 128
+    chunk = 256
     chunks = length // chunk
     dma = pltpu.SemaphoreType.DMA
     hbm = pl.BlockSpec(memory_space=pl.ANY)

time: 19.2 us -> 17.8 us (0.927)
  Pallas kernels: 17.8 us -> 16.4 us
    pallas_call x1, Pallas kernels: 17.8 us -> 16.4 us  [on_device(): pl.pallas_call(functools.partial(kernel, n, chunk), out_shape=jax.ShapeDt...]
where the time goes in v2:
time: 17.8 us; the launch traced here: 17.7 us
  Pallas kernels  16.4 us (92%)
  local copies, waits for them, and re-layouts  1.24 us (7%)
    pallas_call x1, Pallas kernels, on_device(): pl.pallas_call(functools.partial(kernel, n, chunk), out_shape=jax.ShapeDt...  16.4 us
    unnamed x1, local copies, waits for them, and re-layouts  1.24 us

profile of v2, /device:TPU:0, one launch (start us, length us, event | category | flops | bytes accessed | tf_op | source)
XLA Modules:
  0.0 17.7 jit_solution(439391948313228612)
XLA Ops:
  0.0 16.4 %shard_map.100 = f32[2,16]{1,0:T(2,128)} custom-call(bf16[2,256,7168]{2,1,0:T(8,128)(2,1)} %th.1, bf16[2,256,2048]{2,1,0:T(8,128)(2,1)} %tg.1, s32[2]{0:T(128)} %tp.1, bf16[2,64,7168]{2,1,0:T(8,128)(2,1)} %qh.1, bf16[2,64,2048]{2,1,0:T(8,128)(2,1)} %qg.1, s32[2]{0:T(128)} %qp.1, bf16[64,7168]{1,0:T(8,128)(2,1)} %pi.1, bf16[64,2048]{1,0:T(8,128)(2,1)} %po.1, ...), custom_call_target="tpu_custom_call" | custom-call | flops 754974720 | bytes 11796480 | tf_op jit(solution)/shard_map/pallas_call | solution.py:200
  16.4 1.2 %copy.12 = f32[2,16]{1,0:T(2,128)} copy(f32[2,16]{1,0:T(2,128)} %shard_map.100) | data formatting | bytes 256

commit v3 on v2

--- a/solution.py
+++ b/solution.py
@@ -154,10 +154,13 @@
         ex_o.append(send(o_send.at[s], o_recv.at[s], o_ssem.at[s], o_rsem.at[s], {"tensor": other}))
 
     ex_i = []
+    for copy in load_th:
+        copy.wait()
+    both = dot(th_v[...].reshape(seqs * length, -1), pi_v[...], NT)
     for s in range(seqs):
         for j in range(chunks):
-            load_th[s * chunks + j].wait()
-            i_send[s, j] = pack(dot(th_v[s, pl.ds(j * chunk, chunk), :], pi_v[...], NT))
+            first_row = s * length + j * chunk
+            i_send[s, j] = pack(both[first_row : first_row + chunk])
             ex_i.append(
                 send(i_send.at[s, j], i_recv.at[s, j], i_ssem.at[s, j], i_rsem.at[s, j], {"tensor": other})
             )

time: 17.8 us -> 16.7 us (0.938)
  Pallas kernels: 16.4 us -> 15.2 us
    pallas_call x1, Pallas kernels: 16.4 us -> 15.2 us  [on_device(): pl.pallas_call(functools.partial(kernel, n, chunk), out_shape=jax.ShapeDt...]
where the time goes in v3:
time: 16.7 us; the launch traced here: 16.4 us
  Pallas kernels  15.2 us (91%)
  local copies, waits for them, and re-layouts  1.24 us (7%)
    pallas_call x1, Pallas kernels, on_device(): pl.pallas_call(functools.partial(kernel, n, chunk), out_shape=jax.ShapeDt...  15.2 us
    unnamed x1, local copies, waits for them, and re-layouts  1.24 us

profile of v3, /device:TPU:0, one launch (start us, length us, event | category | flops | bytes accessed | tf_op | source)
XLA Modules:
  0.0 16.4 jit_solution(4356342063358680939)
XLA Ops:
  0.0 15.2 %shard_map.100 = f32[2,16]{1,0:T(2,128)} custom-call(bf16[2,256,7168]{2,1,0:T(8,128)(2,1)} %th.1, bf16[2,256,2048]{2,1,0:T(8,128)(2,1)} %tg.1, s32[2]{0:T(128)} %tp.1, bf16[2,64,7168]{2,1,0:T(8,128)(2,1)} %qh.1, bf16[2,64,2048]{2,1,0:T(8,128)(2,1)} %qg.1, s32[2]{0:T(128)} %qp.1, bf16[64,7168]{1,0:T(8,128)(2,1)} %pi.1, bf16[64,2048]{1,0:T(8,128)(2,1)} %po.1, ...), custom_call_target="tpu_custom_call" | custom-call | flops 754974720 | bytes 11796480 | tf_op jit(solution)/shard_map/pallas_call | solution.py:203
  15.2 1.2 %copy.12 = f32[2,16]{1,0:T(2,128)} copy(f32[2,16]{1,0:T(2,128)} %shard_map.100) | data formatting | bytes 256

commit v4 on v3

--- a/solution.py
+++ b/solution.py
@@ -105,14 +105,8 @@
     load_pi.wait()
     load_qh.wait()
     load_tg = load(tg, tg_v, 8)
-    load_th = []
-    for s in range(seqs):
-        for j in range(chunks):
-            rows = pl.ds(j * chunk, chunk)
-            copy = pltpu.make_async_copy(th.at[s, rows], th_v.at[s, rows], h_sem.at[s, j])
-            copy.start()
-            load_th.append(copy)
-
+    load_th = [pltpu.make_async_copy(th, th_v, h_sem.at[0, 0])]
+    load_th[0].start()
     q_in = dot(qh_v[...].reshape(queries * q_length, -1), pi_v[...], NT)
     q_both = jnp.concatenate([q_in, q_out], axis=1)
     first, second = q_both[:q_length], q_both[q_length:]
@@ -149,8 +143,9 @@
 
     load_tg.wait()
     ex_o = []
-    for s in range(seqs):
-        o_send[s] = pack(dot(tg_v[s], po_v[...], NT))
+    both_out = dot(tg_v[...].reshape(seqs * length, -1), po_v[...], NT)
+    for s in range(seqs):
+        o_send[s] = pack(both_out[s * length : (s + 1) * length])
         ex_o.append(send(o_send.at[s], o_recv.at[s], o_ssem.at[s], o_rsem.at[s], {"tensor": other}))
 
     ex_i = []

time: 16.7 us -> 16.7 us (level)
  no operation moved by 1% of the time
where the time goes in v4:
time: 16.7 us; the launch traced here: 16.4 us
  Pallas kernels  15.2 us (91%)
  local copies, waits for them, and re-layouts  1.24 us (7%)
    pallas_call x1, Pallas kernels, on_device(): pl.pallas_call(functools.partial(kernel, n, chunk), out_shape=jax.ShapeDt...  15.2 us
    unnamed x1, local copies, waits for them, and re-layouts  1.24 us

profile of v4, /device:TPU:0, one launch (start us, length us, event | category | flops | bytes accessed | tf_op | source)
XLA Modules:
  0.0 16.4 jit_solution(7645450705391614593)
XLA Ops:
  0.0 15.2 %shard_map.100 = f32[2,16]{1,0:T(2,128)} custom-call(bf16[2,256,7168]{2,1,0:T(8,128)(2,1)} %th.1, bf16[2,256,2048]{2,1,0:T(8,128)(2,1)} %tg.1, s32[2]{0:T(128)} %tp.1, bf16[2,64,7168]{2,1,0:T(8,128)(2,1)} %qh.1, bf16[2,64,2048]{2,1,0:T(8,128)(2,1)} %qg.1, s32[2]{0:T(128)} %qp.1, bf16[64,7168]{1,0:T(8,128)(2,1)} %pi.1, bf16[64,2048]{1,0:T(8,128)(2,1)} %po.1, ...), custom_call_target="tpu_custom_call" | custom-call | flops 754974720 | bytes 11796480 | tf_op jit(solution)/shard_map/pallas_call | solution.py:198
  15.2 1.2 %copy.12 = f32[2,16]{1,0:T(2,128)} copy(f32[2,16]{1,0:T(2,128)} %shard_map.100) | data formatting | bytes 256
